TPU v7x, 32 devices: a whole 2x2x4 slice. The times are simulated.
32 devices in a mesh: rep: 2 (over core), lists: 16 (over z, y, x).
Axes of the slice: x: 2, y: 2, z: 4, core: 2. Of those that a mesh axis runs over, the one named last changes fastest.
Arguments:
- queries: bfloat16 [4096, 768], P(('rep', 'lists')), may hold values from -6 to 6
- rates: bfloat16 [4096], P(('rep', 'lists')), may hold values from 1.9967556e-06 to 4.9829483e-05
- probes: int32 [4096, 8], P(('rep', 'lists')), may hold values from 0 to 31, all different within a row; in each aligned block of 128 rows (0 to 127, 128 to 255, ...) at most 64 rows name the same one
- list_place: int32 [32], replicated, may hold values from 0 to 31, each once
- items: bfloat16 [65536, 768], P('lists'), may hold values from -0.21875 to 0.21875
- ages: int32 [65536], P('lists'), may hold values from 0 to 86399
- fresh_items: bfloat16 [32768, 768], P(('rep', 'lists')), may hold values from -0.21875 to 0.21875
- fresh_ages: int32 [32768], P(('rep', 'lists')), may hold values from 0 to 7199
- owner: int32 [1], replicated, may hold values from 0 to 31
Outputs:
- block_max: float32 [4096, 128], P(('rep', 'lists'))
- fresh_max: float32 [4096, 8], P(('rep', 'lists'))
Inputs may be any that keep to these rules, and one draw needn't show every extreme that they name: `probes`: within the rows of one device (aligned blocks of 128 queries) no list is probed by more than 64 queries; the 8 lists of a query differ. `list_place`: each slot once.
All inputs are finite; a program needn't handle non-finite values.
Results may differ from a plain program's by a relative error of at most 0.0003.
Values may be sent and summed in bfloat16 or wider, within the bound.
A program may use at most 128 MiB of HBM per device.

v0:
```python
import jax
import jax.numpy as jnp
from jax import lax
from jax.sharding import PartitionSpec as P

ITEMS_BLOCK = 128


def broadcast(shard, axis, root):
    mine = lax.axis_index(axis) == root
    return lax.psum(jnp.where(mine, shard, jnp.zeros_like(shard)), axis)


def block_best(rows, row_rates, item_rows, item_ages):
    dots = lax.dot_general(
        rows, item_rows, (((1,), (1,)), ((), ())), preferred_element_type=jnp.float32
    )
    decay = jnp.exp(
        -row_rates.astype(jnp.float32)[:, None] * item_ages.astype(jnp.float32)[None, :]
    )
    scored = dots * decay
    return jnp.max(scored.reshape(rows.shape[0], -1, ITEMS_BLOCK), axis=2)


def score_lists(queried, rated, item_rows, item_ages):
    results = []
    for slot in range(queried.shape[1]):
        rows = queried[:, slot].reshape(-1, queried.shape[3])
        row_rates = rated[:, slot].reshape(-1)
        best = block_best(rows, row_rates, item_rows[slot], item_ages[slot])
        results.append(best.reshape(queried.shape[0], queried.shape[2], -1))
    return jnp.stack(results, axis=1)


def send_back(best):
    return lax.all_to_all(best, "lists", split_axis=0, concat_axis=0, tiled=True)


def shards(queries, rates, probes, list_place, items, ages, fresh_items, fresh_ages, owner):
    q_dev = queries.shape[0]
    width = queries.shape[1]
    probe_count = probes.shape[1]
    list_total = list_place.shape[0]
    peers = lax.axis_size("lists")
    per_dev = list_total // peers
    list_rows = items.shape[0] // per_dev
    most = max(2, (2 * q_dev * probe_count + list_total - 1) // list_total)
    slots_total = list_total * most
    per_block = q_dev * probe_count
    item_rows = items.reshape(per_dev, list_rows, width)
    item_ages = ages.reshape(per_dev, list_rows)
    lists_iota = jnp.arange(list_total, dtype=jnp.int32)
    flat = probes.reshape(-1)
    where_to = jnp.sum(
        jnp.where(flat[:, None] == lists_iota[None, :], list_place[None, :], 0), axis=1
    )
    onehot = (where_to[:, None] == lists_iota[None, :]).astype(jnp.int32)
    earlier = jnp.cumsum(onehot, axis=0) - onehot
    rank = jnp.sum(earlier * onehot, axis=1)
    target = where_to * most + rank
    row_of = (
        jnp.full((slots_total,), per_block, jnp.int32)
        .at[target]
        .set(jnp.arange(per_block, dtype=jnp.int32))
    )
    padded_q = jnp.concatenate([queries, jnp.zeros((1, width), queries.dtype)], axis=0)
    padded_r = jnp.concatenate([rates, jnp.zeros((1,), rates.dtype)], axis=0)
    picked = row_of // probe_count
    send_q = jnp.take(padded_q, picked, axis=0).reshape(peers, per_dev, most, width)
    send_r = jnp.take(padded_r, picked, axis=0).reshape(peers, per_dev, most)
    returned = send_back(
        score_lists(
            lax.all_to_all(send_q, "lists", split_axis=0, concat_axis=0, tiled=True),
            lax.all_to_all(send_r, "lists", split_axis=0, concat_axis=0, tiled=True),
            item_rows,
            item_ages,
        )
    )
    answers = returned.reshape(slots_total, -1)
    block_max = jnp.take(answers, target, axis=0).reshape(q_dev, -1)
    fresh, fresh_age = (
        broadcast(fresh_items, ("rep", "lists"), owner[0]),
        broadcast(fresh_ages, ("rep", "lists"), owner[0]),
    )
    fresh_max = block_best(queries, rates, fresh, fresh_age)
    return (block_max, fresh_max)


def solution(mesh):
    placed = (
        P(("rep", "lists"), None),
        P(("rep", "lists")),
        P(("rep", "lists"), None),
        P(),
        P("lists", None),
        P("lists"),
        P(("rep", "lists"), None),
        P(("rep", "lists")),
        P(),
    )
    return jax.shard_map(
        shards,
        mesh=mesh,
        in_specs=placed,
        out_specs=(P(("rep", "lists"), None), P(("rep", "lists"), None)),
        check_vma=False,
    )
```

profile of v0, /device:TPU:0, one launch (start us, length us, event | category | flops | bytes accessed | tf_op | source)
XLA Modules:
  0.0 248.4 jit_solution(11439031994687798306)
XLA Ops:
  7.2 0.8 copy.33
  8.0 0.1 eq.42
  8.1 0.7 select_reduce_fusion
  8.9 9.0 %reduce-window.6 = s32[32,8,128]{2,1,0:T(8,128)S(1)} reduce-window(s32[32,8,128]{2,1,0:T(8,128)S(1)} %fusion.6, s32[]{:T(128)} %constant.47.clone.1), window={size=1x1x128 pad=0_0x0_0x127_0}, to_apply=%region_1.2 | reduce-window | flops 4161536 | bytes 262148 | tf_op jit(solution)/shard_map/reduce-window
  17.9 0.1 slice.50
  18.0 0.1 copy.34
  18.1 0.1 copy.35
  18.2 0.1 broadcast_add_fusion
  18.4 4.3 %scatter_custom_fusion = s32[2048]{0:T(1024)S(1)} fusion(s32[1024]{0:T(1024)S(1)} %bitcast.66, s32[1024]{0:T(1024)S(1)} %iota.11, s32[]{:T(128)} %constant.71.clone.1), kind=kCustom, calls=%fused_computation.47 | custom fusion | bytes 8196 | tf_op jit(solution)/shard_map/scatter | solution.py:64
  22.8 0.7 pad_maximum_fusion.1
  23.5 12.5 %gather_fusion.1 = bf16[2048]{0:T(1024)(128)(2,1)S(1)} fusion(bf16[129]{0:T(256)(128)(2,1)S(1)} %pad_maximum_fusion.1, s32[2048]{0:T(1024)S(1)} %broadcast_clamp_fusion), kind=kCustom, calls=%fused_computation.1 | custom fusion | bytes 16384 | tf_op jit(solution)/shard_map/jit(_take)/gather | solution.py:70
  36.0 0.1 gather.21
  36.0 0.1 broadcast_in_dim.67
  36.1 0.6 broadcast_select_fusion.2
  36.7 8.4 %all-to-all-start.1 = ((bf16[16,2,64]{2,1,0:T(2,128)(2,1)}), bf16[16,2,64]{2,1,0:T(2,128)(2,1)}, u32[]{:S(2)}, u32[]{:S(2)}) async-start(bf16[16,2,64]{2,1,0:T(2,128)(2,1)} %broadcast_select_fusion.2), calls=%async_computation.1 | async-start | bytes 16384 | tf_op jit(solution)/shard_map/all_to_all | solution.py:74
  45.2 8.6 %gather_fusion = bf16[2048,768]{1,0:T(8,128)(2,1)S(1)} fusion(bf16[129,768]{1,0:T(8,128)(2,1)S(1)} %concatenate.6, s32[2048]{0:T(1024)} %copy-done.3), kind=kCustom, calls=%fused_computation | custom fusion | bytes 6299648 | tf_op jit(solution)/shard_map/jit(_take)/gather | solution.py:69
  53.8 2.6 %broadcast_select_fusion = bf16[16,2,64,768]{3,2,1,0:T(8,128)(2,1)} fusion(bf16[16,2,64,768]{3,2,1,0:T(8,128)(2,1)S(1)} %bitcast.56, pred[16,2,64]{2,1,0:T(4,128)(4,1)} %copy-done.2), kind=kLoop, calls=%fused_computation.8 | loop fusion | flops 1572864 | bytes 6293504 | tf_op jit(solution)/shard_map/jit(_take)/select_n | solution.py:69
  56.3 6.9 %all-to-all-start = ((bf16[16,2,64,768]{3,2,1,0:T(8,128)(2,1)}), bf16[16,2,64,768]{3,2,1,0:T(8,128)(2,1)S(1)}, u32[]{:S(2)}, u32[]{:S(2)}) async-start(bf16[16,2,64,768]{3,2,1,0:T(8,128)(2,1)} %broadcast_select_fusion), calls=%async_computation | async-start | bytes 6291456 | tf_op jit(solution)/shard_map/all_to_all | solution.py:73
  63.2 0.2 all-reduce.3.cloned.1.call-start
  64.1 1.3 broadcast_select_fusion.1
  65.4 0.1 add.67
  65.6 0.8 fusion.11
  66.4 0.1 neg.27
  66.5 0.1 neg.29
  66.6 64.4 %all-to-all-done = bf16[16,2,64,768]{3,2,1,0:T(8,128)(2,1)S(1)} async-done(((bf16[16,2,64,768]{3,2,1,0:T(8,128)(2,1)}), bf16[16,2,64,768]{3,2,1,0:T(8,128)(2,1)S(1)}, u32[]{:S(2)}, u32[]{:S(2)}) %all-to-all-start) | async-done | bytes 3145760 | tf_op jit(solution)/shard_map/all_to_all | solution.py:73
  130.9 1.4 fusion.15
  132.3 5.4 %multiply_bitcast_fusion = f32[128,8,16,128]{3,1,2,0:T(8,128)S(1)} fusion(bf16[1024,768]{1,0:T(8,128)(2,1)S(1)} %bitcast.60, f32[2048]{0:T(1024)S(1)} %get-tuple-element.15, f32[1024]{0:T(1024)S(1)} %neg.29, bf16[4096,768]{1,0:T(8,128)(2,1)} %param.13), kind=kOutput, calls=%fused_computation.4 | convolution fusion | flops 3225419776 | bytes 13119488 | tf_op jit(solution)/shard_map/dot_general | solution.py:15
  137.7 5.2 %copy.50 = f32[128,8,16,128]{3,2,1,0:T(8,128)} copy(f32[128,8,16,128]{3,1,2,0:T(8,128)S(1)} %multiply_bitcast_fusion) | data formatting | bytes 16777216
  142.9 5.8 %reduce_max.28 = f32[1024,16]{1,0:T(8,128)S(1)} reduce(f32[1024,16,128]{2,1,0:T(8,128)} %bitcast.54, f32[]{:T(128)} %constant.81.clone.1), dimensions={2}, to_apply=%region_6.7 | reduce | flops 2080768 | bytes 8454148 | tf_op jit(solution)/shard_map/reduce_max | solution.py:22
  148.7 0.2 copy.40
  148.9 5.4 %multiply_bitcast_fusion.1 = f32[128,8,16,128]{3,1,2,0:T(8,128)S(1)} fusion(bf16[1024,768]{1,0:T(8,128)(2,1)S(1)} %bitcast.59, f32[2048]{0:T(1024)S(1)} %get-tuple-element.14, f32[1024]{0:T(1024)S(1)} %neg.27, bf16[4096,768]{1,0:T(8,128)(2,1)} %param.13), kind=kOutput, calls=%fused_computation.5 | convolution fusion | flops 3225419776 | bytes 13119488 | tf_op jit(solution)/shard_map/dot_general | solution.py:15
  154.2 5.2 %copy.49 = f32[128,8,16,128]{3,2,1,0:T(8,128)} copy(f32[128,8,16,128]{3,1,2,0:T(8,128)S(1)} %multiply_bitcast_fusion.1) | data formatting | bytes 16777216
  159.5 5.9 %reduce_max.27 = f32[1024,16]{1,0:T(8,128)S(1)} reduce(f32[1024,16,128]{2,1,0:T(8,128)} %bitcast.53, f32[]{:T(128)} %constant.81.clone.1), dimensions={2}, to_apply=%region_5.6 | reduce | flops 2080768 | bytes 8454148 | tf_op jit(solution)/shard_map/reduce_max | solution.py:22
  165.4 0.2 copy.39
  165.6 0.8 reshape.181
  166.4 15.8 %all-to-all-start.2 = ((f32[16,1,2048]{2,1,0:T(1,128)}), f32[16,1,2048]{2,1,0:T(1,128)S(1)}, u32[]{:S(2)}, u32[]{:S(2)}) async-start(f32[16,1,2048]{2,1,0:T(1,128)} %reshape.181), calls=%async_computation.2 | async-start | bytes 262144 | tf_op jit(solution)/shard_map/all_to_all | solution.py:36
  182.3 40.7 %psum.15 = s32[1024]{0:T(1024)S(1)} all-reduce(s32[1024]{0:T(1024)S(1)} %broadcast_select_fusion.3), channel_id=1, replica_groups=mesh['rep'=2,'lists'=16] {'rep','lists'}, use_global_device_ids=true, to_apply=%region_8.9 | all-reduce | flops 1024 | bytes 8192 | tf_op jit(solution)/shard_map/psum | solution.py:11
  223.0 0.1 copy.36
  223.1 10.1 %all-reduce.3.cloned.1.call-done = bf16[1024,768]{1,0:T(8,128)(2,1)} async-done(((bf16[1024,768]{1,0:T(8,128)(2,1)}), bf16[1024,768]{1,0:T(8,128)(2,1)}) %all-reduce.3.cloned.1.call-update) | async-done | bytes 1572880 | tf_op jit(solution)/shard_map/psum | solution.py:11
  233.2 2.6 %bitcast_reduce_fusion = f32[128,8]{0,1:T(8,128)} fusion(bf16[1024,768]{1,0:T(8,128)(2,1)} %all-reduce.3.cloned.1.call-done, bf16[128,768]{1,0:T(8,128)(2,1)S(1)} %copy-done.1, f32[1024]{0:T(1024)S(1)} %convert_element_type.46, f32[128]{0:T(128)S(1)} %convert_negate_fusion), kind=kOutput, calls=%fused_computation.12 | convolution fusion | flops 201718784 | bytes 1778176 | tf_op jit(solution)/shard_map/dot_general | solution.py:15
  235.8 0.5 broadcast.103
  236.3 0.9 reduce.8
  237.2 0.1 reshape.182
  237.3 0.3 copy.41
  237.7 2.8 %gather_fusion.2 = f32[1024,16]{1,0:T(8,128)S(1)} fusion(f32[2048,16]{1,0:T(8,128)S(1)} %bitcast.55, s32[1024]{0:T(1024)S(1)} %broadcast_clamp_fusion.1), kind=kCustom, calls=%fused_computation.2 | custom fusion | bytes 135168 | tf_op jit(solution)/shard_map/jit(_take)/gather | solution.py:80
  240.5 0.2 gather.23
  240.7 0.1 copy.42
  240.8 0.7 copy.43
  (39 shorter events, 0.3 us)
Async XLA Ops:
  7.2 38.0 %copy-start.1 = (bf16[128,768]{1,0:T(8,128)(2,1)S(1)}, bf16[128,768]{1,0:T(8,128)(2,1)}, u32[]{:S(2)}) copy-start(bf16[128,768]{1,0:T(8,128)(2,1)} %param.9) | copy-start | bytes 589828
  18.4 4.3 %copy-start.5 = (s32[1024,1]{0,1:T(1,128)}, s32[1024,1]{0,1:T(1,128)S(1)}, u32[]{:S(2)}) copy-start(s32[1024,1]{0,1:T(1,128)S(1)} %compare_select_fusion.1) | copy-start | bytes 12292
  22.8 22.3 %copy-start.3 = (s32[2048]{0:T(1024)}, s32[2048]{0:T(1024)S(1)}, u32[]{:S(2)}) copy-start(s32[2048]{0:T(1024)S(1)} %broadcast_clamp_fusion) | copy-start | bytes 24580
  36.1 9.0 %copy-start.2 = (pred[16,2,64]{2,1,0:T(4,128)(4,1)}, pred[16,2,64]{2,1,0:T(4,128)(4,1)S(1)}, u32[]{:S(2)}) copy-start(pred[16,2,64]{2,1,0:T(4,128)(4,1)S(1)} %broadcast_in_dim.67) | copy-start | bytes 6148
  36.7 19.6 %all-to-all-start.1 = ((bf16[16,2,64]{2,1,0:T(2,128)(2,1)}), bf16[16,2,64]{2,1,0:T(2,128)(2,1)}, u32[]{:S(2)}, u32[]{:S(2)}) async-start(bf16[16,2,64]{2,1,0:T(2,128)(2,1)} %broadcast_select_fusion.2), calls=%async_computation.1 | async-start | bytes 16384 | tf_op jit(solution)/shard_map/all_to_all | solution.py:74
  56.3 74.6 %all-to-all-start = ((bf16[16,2,64,768]{3,2,1,0:T(8,128)(2,1)}), bf16[16,2,64,768]{3,2,1,0:T(8,128)(2,1)S(1)}, u32[]{:S(2)}, u32[]{:S(2)}) async-start(bf16[16,2,64,768]{3,2,1,0:T(8,128)(2,1)} %broadcast_select_fusion), calls=%async_computation | async-start | bytes 6291456 | tf_op jit(solution)/shard_map/all_to_all | solution.py:73
  63.2 2.3 copy-start.6
  63.2 2.3 copy-start.7
  63.2 2.3 copy-start.4
  63.2 169.9 %all-reduce.3.cloned.1.call-start = ((), (), s32[]{:S(2)}) async-start(), calls=%async_computation.3 | async-start | bytes 3145728 | tf_op jit(solution)/shard_map/psum | solution.py:11
  142.9 6.0 %copy-start = (bf16[16,1,64,768]{3,2,1,0:T(8,128)(2,1)S(1)}, bf16[16,1,64,768]{3,2,1,0:T(8,128)(2,1)}, u32[]{:S(2)}) copy-start(bf16[16,1,64,768]{3,2,1,0:T(8,128)(2,1)} %get-tuple-element.12) | copy-start | bytes 4718596
  159.5 22.8 %copy-start.8 = (bf16[128]{0:T(256)(128)(2,1)S(1)}, bf16[128]{0:T(256)(128)(2,1)}, u32[]{:S(2)}) copy-start(bf16[128]{0:T(256)(128)(2,1)} %param.10) | copy-start | bytes 772
  166.4 69.3 %all-to-all-start.2 = ((f32[16,1,2048]{2,1,0:T(1,128)}), f32[16,1,2048]{2,1,0:T(1,128)S(1)}, u32[]{:S(2)}, u32[]{:S(2)}) async-start(f32[16,1,2048]{2,1,0:T(1,128)} %reshape.181), calls=%async_computation.2 | async-start | bytes 262144 | tf_op jit(solution)/shard_map/all_to_all | solution.py:36
Sparse Core Ops, SparseCore 0:
  69.4 163.7 all-reduce.2
where the time goes:
time: 249 us; the launch traced here: 248 us
  waiting for transfers between devices  74.5 us (30%)
  local copies, waits for them, and re-layouts  44.9 us (18%)
  blocking collectives  40.7 us (16%)
  starting transfers between devices  31.3 us (13%)
  other arithmetic  28.7 us (12%)
  between operations  15.1 us (6%)
  matrix products  13.3 us (5%)
    all_to_all x1, waiting for transfers between devices, shards(): lax.all_to_all(send_q, 'lists', split_axis=0, concat_axis=0, tiled=True)  64.4 us
    psum x1, blocking collectives, broadcast(): return lax.psum(jnp.where(mine, shard, jnp.zeros_like(shard)), axis)  40.7 us
    all_to_all x1, starting transfers between devices, send_back(): lax.all_to_all(best, 'lists', split_axis=0, concat_axis=0, tiled=True)  15.8 us
    dot_general x3, matrix products, block_best(): lax.dot_general(rows, item_rows, (((1,), (1,)), ((), ())), preferred_elem...  13.3 us
    unnamed x24, local copies, waits for them, and re-layouts  13 us
    gather x2, local copies, waits for them, and re-layouts, shards(): send_r = jnp.take(padded_r, picked, axis=0).reshape(peers, per_dev, most)  12.5 us
    reduce_max x2, other arithmetic, block_best(): return jnp.max(scored.reshape(rows.shape[0], -1, ITEMS_BLOCK), axis=2)  11.7 us
    psum x1, waiting for transfers between devices, broadcast(): return lax.psum(jnp.where(mine, shard, jnp.zeros_like(shard)), axis)  10.1 us
  transfers between devices with their start and end apart: 4, of which 2 were waited for; matrix products, arithmetic and copies ran while one was open for 21% of the time, Pallas kernels for 0%

commit v1 on v0

v1 whole, which is shorter than its diff:
```python
import functools
import math

import jax
import jax.numpy as jnp
from jax import lax
from jax.experimental import pallas as pl
from jax.experimental.pallas import tpu as pltpu
from jax.sharding import PartitionSpec as P

ITEMS_BLOCK = 128
CHUNK = 1024
LOG2E = math.log2(math.e)
MESH = pl.DeviceIdType.MESH


def grid_of(n):
    if n == 16:
        return 4, 2, 2
    if n == 128:
        return 4, 4, 8
    return n, 1, 1


def kernel(
    n, dims, lists_n, per_dev,
    owner_ref, place_ref, rates_ref, probes_ref, ages_ref, fages_ref, q_ref, items_ref, fresh_ref,
    out_ref, fout_ref,
    gath, qp, item_v, fresh_v, fage_v, age_v, rate_s, rate_v, slot_v, res, ans,
    s_line, s_b, s_c, s_hb, s_hc, s_res, s_rate, r_q, r_res, r_rate, f_sem, l_sem,
):
    A, B, C = dims
    me = lax.axis_index("lists")
    rep = lax.axis_index("rep")
    a, b, c = me // (B * C), (me // C) % B, me % C
    rows = q_ref.shape[0]
    half = rows // 2
    list_rows = item_v.shape[0] // per_dev
    blocks = list_rows // ITEMS_BLOCK
    main_rows = per_dev * blocks

    def at(j, db, dc):
        return ((a + j) % A) * (B * C) + ((b + db) % B) * C + (c + dc) % C

    def remote(src, dst, ss, rs, to):
        return pltpu.make_async_remote_copy(
            src_ref=src, dst_ref=dst, send_sem=ss, recv_sem=rs,
            device_id=(rep, to), device_id_type=MESH,
        )

    barrier = pltpu.get_barrier_semaphore()

    @pl.loop(1, n)
    def _(i):
        pl.semaphore_signal(barrier, inc=1, device_id=(rep, (me + i) % n), device_id_type=MESH)

    pl.semaphore_signal(barrier, inc=1, device_id=(1 - rep, me), device_id_type=MESH)

    own_q = pltpu.make_async_copy(q_ref, gath.at[me], l_sem.at[0])
    own_items = pltpu.make_async_copy(items_ref, item_v, l_sem.at[1])
    own_fresh = pltpu.make_async_copy(fresh_ref, fresh_v.at[0], l_sem.at[2])
    own_q.start()
    own_items.start()
    own_fresh.start()
    rate_s[...] = jnp.broadcast_to(rates_ref[...].astype(jnp.float32) * (-LOG2E), rate_s.shape)
    pl.semaphore_wait(barrier, n)

    def line_send(j):
        return remote(q_ref, gath.at[me], s_line.at[j], r_q.at[me, 0], at(j, 0, 0))

    def column(j, first):
        s = at(j, 0, 0)
        return q_ref if first else gath.at[s]

    def b_send(j, db, first=False):
        s = at(j, 0, 0)
        return remote(column(j, first), gath.at[s], s_b.at[j, db], r_q.at[s, 0], at(0, db, 0))

    def c_send(j, dc, first=False):
        s = at(j, 0, 0)
        return remote(column(j, first), gath.at[s], s_c.at[j, dc], r_q.at[s, 0], at(0, 0, dc))

    def hb_send(j, dc, db):
        part = gath.at[at(j, 0, dc), pl.ds(0, half)]
        return remote(part, part, s_hb.at[j, dc, db], r_q.at[at(j, 0, dc), 0], at(0, db, 0))

    def hc_send(j, db, dc):
        part = gath.at[at(j, db, 0), pl.ds(half, half)]
        return remote(part, part, s_hc.at[j, db, dc], r_q.at[at(j, db, 0), 1], at(0, 0, dc))

    def res_send(s):
        return remote(res.at[s], ans.at[me], s_res.at[s], r_res.at[me], s)

    def rate_send(i):
        to = (me + i) % n
        return remote(rate_s, rate_v.at[me], s_rate.at[i], r_rate.at[me], to)

    def wait_block(s):
        remote(q_ref, gath.at[s], s_line.at[0], r_q.at[s, 0], me).wait_recv()

    def wait_half(s, k):
        part = gath.at[s, pl.ds(k * half, half)]
        remote(part, part, s_line.at[0], r_q.at[s, k], me).wait_recv()

    sibling = pltpu.make_async_remote_copy(
        src_ref=fresh_ref, dst_ref=fresh_v.at[1], send_sem=f_sem.at[0], recv_sem=f_sem.at[1],
        device_id=(1 - rep, me), device_id_type=MESH,
    )
    sibling_age = pltpu.make_async_remote_copy(
        src_ref=fages_ref, dst_ref=fage_v, send_sem=f_sem.at[2], recv_sem=f_sem.at[3],
        device_id=(1 - rep, me), device_id_type=MESH,
    )

    for dc in range(1, C):
        c_send(0, dc, True).start()
    for db in range(1, B):
        b_send(0, db, True).start()
    for j in range(1, A):
        line_send(j).start()

    @pl.loop(1, n)
    def _(i):
        rate_send(i).start()

    sibling_age.start()
    sibling.start()

    def spread(row):
        return jnp.transpose(jnp.broadcast_to(row.astype(jnp.float32), (ITEMS_BLOCK, ITEMS_BLOCK)))

    @pl.loop(0, main_rows)
    def _(k):
        age_v[pl.ds(pl.multiple_of(k * ITEMS_BLOCK, ITEMS_BLOCK), ITEMS_BLOCK), :] = spread(ages_ref[pl.ds(k, 1), :])

    rate_v[me] = rate_s[...]
    probes = jnp.transpose(probes_ref[...])

    def place_step(l, acc):
        return jnp.where(probes == l, place_ref[l], acc)

    slot_v[...] = lax.fori_loop(0, lists_n, place_step, jnp.zeros_like(probes))
    own_q.wait()
    own_items.wait()
    own_fresh.wait()

    other = (owner_ref[0] // n != rep).astype(jnp.int32)
    fresh_blocks = fresh_ref.shape[0] // ITEMS_BLOCK
    per_chunk = CHUNK // ITEMS_BLOCK

    def finish(dots, base, row0, s0, s1):
        age = age_v[pl.ds(base, CHUNK), :]
        for k, s in enumerate((s0, s1)):
            decay = jnp.exp2(age * rate_v[s, pl.ds(0, 1), :])
            scored = dots[:, k * rows:(k + 1) * rows] * decay
            best = jnp.max(scored.reshape(per_chunk, ITEMS_BLOCK, rows), axis=1)
            res[s, pl.ds(row0, per_chunk), :] = best

    def score(x, base, row0, s0, s1):
        dots = lax.dot_general(
            x, qp[...], (((1,), (1,)), ((), ())), preferred_element_type=jnp.float32
        )
        finish(dots, base, row0, s0, s1)

    pairs = B * C // 2
    front = max(1, C // 2) if pairs > 1 else pairs

    @pl.loop(0, A + 1)
    def _(j):
        @pl.when(j + 1 < A)
        def _():
            wait_block(at(j + 1, 0, 0))
            for dc in range(1, C):
                c_send(j + 1, dc).start()
            for db in range(1, B):
                b_send(j + 1, db).start()

        @pl.when(j < A)
        def _():
            for dc in range(1, C):
                wait_block(at(j, 0, dc))
                for db in range(1, B):
                    hb_send(j, dc, db).start()
            for db in range(1, B):
                wait_block(at(j, db, 0))
                for dc in range(1, C):
                    hc_send(j, db, dc).start()

        @pl.loop(0, pairs)
        def _(t):
            jj = jnp.where(t < front, j, j - 1)

            @pl.when((jj >= 0) & (jj < A))
            def _():
                s = []
                for k in range(2):
                    idx = 2 * t + k
                    db, dc = idx // C, idx % C
                    sk = at(jj, db, dc)
                    s.append(sk)

                    @pl.when((db > 0) & (dc > 0))
                    def _():
                        wait_half(sk, 0)
                        wait_half(sk, 1)

                    @pl.when(sk != me)
                    def _():
                        remote(rate_s, rate_v.at[sk], s_rate.at[0], r_rate.at[sk], me).wait_recv()

                    qp[k * rows:(k + 1) * rows, :] = gath[sk]
                s0, s1 = s

                @pl.loop(0, main_rows // per_chunk)
                def _(m):
                    base = pl.multiple_of(m * CHUNK, CHUNK)
                    score(item_v[pl.ds(base, CHUNK), :], base, pl.multiple_of(m * per_chunk, per_chunk), s0, s1)

                @pl.when((j == 0) & (t == 0))
                def _():
                    sibling.wait_recv()
                    sibling_age.wait_recv()
                    for k in range(fresh_blocks):
                        mine, theirs = fages_ref[k:k + 1, :], fage_v[k:k + 1, :]
                        row0 = (main_rows + k) * ITEMS_BLOCK
                        age_v[row0:row0 + ITEMS_BLOCK, :] = spread(jnp.where(other == 0, mine, theirs))

                score(fresh_v[other], main_rows * ITEMS_BLOCK, main_rows, s0, s1)
                for sk in s:
                    @pl.when(sk != me)
                    def _():
                        res_send(sk).start()

    ans[me] = res[me]

    def collect(i, acc):
        s = (me + i) % n

        @pl.when(s != me)
        def _():
            remote(res.at[s], ans.at[s], s_res.at[s], r_res.at[s], me).wait_recv()

        outs, fr = acc
        for sub in range(per_dev):
            part = ans[s, sub * blocks:(sub + 1) * blocks, :]
            outs = tuple(
                jnp.where(slot_v[p:p + 1, :] == s * per_dev + sub, part, o) for p, o in enumerate(outs)
            )
        fr = jnp.where(owner_ref[0] % n == s, ans[s, main_rows:main_rows + fresh_blocks, :], fr)
        return outs, fr

    zero = jnp.zeros((blocks, rows), jnp.float32)
    outs, fr = lax.fori_loop(
        0, n, collect,
        (tuple(zero for _ in range(probes_ref.shape[1])), jnp.zeros((fresh_blocks, rows), jnp.float32)),
    )
    out_ref[...] = jnp.transpose(jnp.concatenate(outs, axis=0))
    fout_ref[...] = jnp.transpose(fr)

    for j in range(A):
        for dc in range(1, C):
            c_send(j, dc, j == 0).wait_send()
        for db in range(1, B):
            b_send(j, db, j == 0).wait_send()
        if j > 0:
            line_send(j).wait_send()
        for dc in range(1, C):
            for db in range(1, B):
                hb_send(j, dc, db).wait_send()
                hc_send(j, db, dc).wait_send()

    @pl.loop(1, n)
    def _(i):
        rate_send(i).wait_send()
        res_send((me + i) % n).wait_send()

    sibling.wait_send()
    sibling_age.wait_send()


def shards(n, queries, rates, probes, list_place, items, ages, fresh_items, fresh_ages, owner):
    dims = grid_of(n)
    A, B, C = dims
    rows, width = queries.shape
    lists_n = list_place.shape[0]
    per_dev = lists_n // n
    item_n, fresh_n = items.shape[0], fresh_items.shape[0]
    main_rows, fresh_rows = item_n // ITEMS_BLOCK, fresh_n // ITEMS_BLOCK
    res_rows = main_rows + fresh_rows
    bf, f32, i32 = jnp.bfloat16, jnp.float32, jnp.int32
    scratch = [
        ((n, rows, width), bf), ((2 * rows, width), bf), ((item_n, width), bf),
        ((2, fresh_n, width), bf), ((fresh_rows, ITEMS_BLOCK), i32),
        ((item_n + fresh_n, ITEMS_BLOCK), f32), ((8, rows), f32), ((n, 8, rows), f32),
        ((probes.shape[1], rows), i32), ((n, res_rows, rows), f32), ((n, res_rows, rows), f32),
    ]
    used = sum(math.prod(shape) * jnp.dtype(kind).itemsize for shape, kind in scratch)
    dma = pltpu.SemaphoreType.DMA
    smem, vmem, hbm = (pl.BlockSpec(memory_space=m) for m in (pltpu.SMEM, pltpu.VMEM, pl.ANY))
    return pl.pallas_call(
        functools.partial(kernel, n, dims, lists_n, per_dev),
        out_shape=(
            jax.ShapeDtypeStruct((rows, probes.shape[1] * (main_rows // per_dev)), f32),
            jax.ShapeDtypeStruct((rows, fresh_rows), f32),
        ),
        in_specs=[smem, smem, vmem, vmem, vmem, vmem, hbm, hbm, hbm],
        out_specs=(vmem, vmem),
        scratch_shapes=[pltpu.VMEM(shape, kind) for shape, kind in scratch] + [
            dma((A,)), dma((A, B)), dma((A, C)), dma((A, C, B)), dma((A, B, C)),
            dma((n,)), dma((n,)), dma((n, 2)), dma((n,)), dma((n,)), dma((4,)), dma((3,)),
        ],
        compiler_params=pltpu.CompilerParams(
            collective_id=0, has_side_effects=True, vmem_limit_bytes=used + (10 << 20)
        ),
    )(
        owner, list_place, rates.reshape(1, rows), probes,
        ages.reshape(main_rows, ITEMS_BLOCK), fresh_ages.reshape(fresh_rows, ITEMS_BLOCK),
        queries, items, fresh_items,
    )


def solution(mesh):
    placed = (
        P(("rep", "lists"), None),
        P(("rep", "lists")),
        P(("rep", "lists"), None),
        P(),
        P("lists", None),
        P("lists"),
        P(("rep", "lists"), None),
        P(("rep", "lists")),
        P(),
    )
    return jax.shard_map(
        functools.partial(shards, mesh.shape["lists"]),
        mesh=mesh,
        in_specs=placed,
        out_specs=(P(("rep", "lists"), None), P(("rep", "lists"), None)),
        check_vma=False,
    )
```

time: 249 us -> 74.3 us (0.30)
  waiting for transfers between devices: 74.5 us -> 0 us
  Pallas kernels: 0 us -> 62.7 us
  blocking collectives: 40.7 us -> 0 us
  local copies, waits for them, and re-layouts: 44.9 us -> 9.9 us
  starting transfers between devices: 31.3 us -> 0 us
  other arithmetic: 28.7 us -> 0 us
  between operations: 15.1 us -> 1.3 us
  matrix products: 13.3 us -> 0 us
    all_to_all x3 -> x0, waiting for transfers between devices: 64.4 us -> none  [the longest x1 64.4 us: shards(): lax.all_to_all(send_q, 'lists', split_axis=0, concat_axis=0, tiled=True)]
    pallas_call x0 -> x1, Pallas kernels: none -> 62.7 us  [shards(): pl.pallas_call(functools.partial(kernel, n, dims, lists_n, per_dev), out_...]
    psum x1 -> x0, blocking collectives: 40.7 us -> none  [broadcast(): return lax.psum(jnp.where(mine, shard, jnp.zeros_like(shard)), axis)]
    all_to_all x3 -> x0, starting transfers between devices: 31 us -> none  [the longest x1 15.8 us: send_back(): lax.all_to_all(best, 'lists', split_axis=0, concat_axis=0, tiled=True)]
    gather x6 -> x0, local copies, waits for them, and re-layouts: 24.2 us -> none  [the longest x2 12.5 us: shards(): send_r = jnp.take(padded_r, picked, axis=0).reshape(peers, per_dev, most)]
    dot_general x3 -> x0, matrix products: 13.3 us -> none  [block_best(): lax.dot_general(rows, item_rows, (((1,), (1,)), ((), ())), preferred_elem...]
    reduce_max x2 -> x0, other arithmetic: 11.7 us -> none  [block_best(): return jnp.max(scored.reshape(rows.shape[0], -1, ITEMS_BLOCK), axis=2)]
    psum x1 -> x0, waiting for transfers between devices: 10.1 us -> none  [broadcast(): return lax.psum(jnp.where(mine, shard, jnp.zeros_like(shard)), axis)]
  transfers between devices with their start and end apart: 4 -> 0, of which waited for: 2 -> 0; matrix products, arithmetic and copies ran while one was open for 21% -> 0% of each run, Pallas kernels for 0% -> 0%
where the time goes in v1:
time: 74.3 us; the launch traced here: 73.9 us
  Pallas kernels  62.7 us (84%)
  local copies, waits for them, and re-layouts  9.9 us (13%)
  between operations  1.3 us (2%)
    pallas_call x1, Pallas kernels, shards(): pl.pallas_call(functools.partial(kernel, n, dims, lists_n, per_dev), out_...  62.7 us
    unnamed x16, local copies, waits for them, and re-layouts  9.24 us

profile of v1, /device:TPU:0, one launch (start us, length us, event | category | flops | bytes accessed | tf_op | source)
XLA Modules:
  0.0 73.9 jit_solution(2614541248584844248)
XLA Ops:
  1.3 0.8 %copy.11.probes_ref = s32[128,8]{1,0:T(8,128)S(1)} copy(s32[128,8]{0,1:T(8,128)} %param.11) | data formatting | bytes 8192 | tf_op args[2]
  2.1 0.0 copy-start
  2.1 2.8 %copy-done = bf16[4096,768]{1,0:T(8,128)(2,1)S(1)} copy-done((bf16[4096,768]{1,0:T(8,128)(2,1)S(1)}, bf16[4096,768]{1,0:T(8,128)(2,1)}, u32[]{:S(2)}) %copy-start) | copy-done | bytes 6291480
  4.8 0.0 copy-start.1
  4.9 1.4 %copy-done.1 = bf16[1024,768]{1,0:T(8,128)(2,1)S(1)} copy-done((bf16[1024,768]{1,0:T(8,128)(2,1)S(1)}, bf16[1024,768]{1,0:T(8,128)(2,1)}, u32[]{:S(2)}) %copy-start.1) | copy-done | bytes 1572888
  6.3 0.0 copy-start.2
  6.3 0.9 %copy-done.2 = bf16[128,768]{1,0:T(8,128)(2,1)S(1)} copy-done((bf16[128,768]{1,0:T(8,128)(2,1)S(1)}, bf16[128,768]{1,0:T(8,128)(2,1)}, u32[]{:S(2)}) %copy-start.2) | copy-done | bytes 196632
  7.2 0.0 copy-start.3
  7.2 0.7 copy-done.3
  7.9 0.0 copy-start.4
  7.9 0.7 copy-done.4
  8.6 0.0 copy-start.5
  8.6 0.7 copy-done.5
  9.2 0.0 copy-start.6
  9.2 0.7 copy-done.6
  9.9 62.7 %shard_map.104 = (f32[128,128]{1,0:T(8,128)S(1)}, f32[128,8]{1,0:T(8,128)S(1)}) custom-call(s32[1]{0:T(128)S(6)} %copy.14.owner_ref, s32[32]{0:T(128)S(1)} %copy-done.5, bf16[1,128]{1,0:T(2,128)(2,1)S(1)} %bitcast.5, s32[128,8]{1,0:T(8,128)S(1)} %copy.11.probes_ref, s32[32,128]{1,0:T(8,128)S(1)} %bitcast.3, s32[8,128]{1,0:T(8,128)S(1)} %bitcast.4, ...), custom_call_target="tpu_custom_call" | custom-call | tf_op jit(solution)/shard_map/pallas_call | solution.py:299
  72.6 0.7 copy.12
  73.3 0.6 copy.15
Async XLA Ops:
  2.1 2.8 %copy-start = (bf16[4096,768]{1,0:T(8,128)(2,1)S(1)}, bf16[4096,768]{1,0:T(8,128)(2,1)}, u32[]{:S(2)}) copy-start(bf16[4096,768]{1,0:T(8,128)(2,1)} %items_ref.1) | copy-start | bytes 18874372
  4.8 1.4 %copy-start.1 = (bf16[1024,768]{1,0:T(8,128)(2,1)S(1)}, bf16[1024,768]{1,0:T(8,128)(2,1)}, u32[]{:S(2)}) copy-start(bf16[1024,768]{1,0:T(8,128)(2,1)} %fresh_ref.1) | copy-start | bytes 4718596
  6.3 0.9 %copy-start.2 = (bf16[128,768]{1,0:T(8,128)(2,1)S(1)}, bf16[128,768]{1,0:T(8,128)(2,1)}, u32[]{:S(2)}) copy-start(bf16[128,768]{1,0:T(8,128)(2,1)} %q_ref.1) | copy-start | bytes 589828
  7.2 0.7 copy-start.3
  7.9 0.7 copy-start.4
  8.6 0.7 copy-start.5
  9.2 0.7 copy-start.6

commit v2 on v1

--- a/solution.py
+++ b/solution.py
@@ -24,9 +24,9 @@
 
 def kernel(
     n, dims, lists_n, per_dev,
-    owner_ref, place_ref, rates_ref, probes_ref, ages_ref, fages_ref, q_ref, items_ref, fresh_ref,
+    owner_ref, place_ref, rates_ref, probes_hbm, ages_hbm, fages_hbm, q_ref, items_ref, fresh_ref,
     out_ref, fout_ref,
-    gath, qp, item_v, fresh_v, fage_v, age_v, rate_s, rate_v, slot_v, res, ans,
+    gath, qp, item_v, fresh_v, fage_v, age_v, rate_s, rate_v, slot_v, res, ans, probes_ref, ages_ref, fages_ref,
     s_line, s_b, s_c, s_hb, s_hc, s_res, s_rate, r_q, r_res, r_rate, f_sem, l_sem,
 ):
     A, B, C = dims
@@ -39,8 +39,13 @@
     blocks = list_rows // ITEMS_BLOCK
     main_rows = per_dev * blocks
 
+    def along(j):
+        if A % 4:
+            return (a + j) % A
+        return (a // 4 * 4 + j // 4 * 4) % A + (a // 2 + j // 2) % 2 * 2 + (a + j) % 2
+
     def at(j, db, dc):
-        return ((a + j) % A) * (B * C) + ((b + db) % B) * C + (c + dc) % C
+        return along(j) * (B * C) + ((b + db) % B) * C + (c + dc) % C
 
     def remote(src, dst, ss, rs, to):
         return pltpu.make_async_remote_copy(
@@ -59,6 +64,12 @@
     own_q = pltpu.make_async_copy(q_ref, gath.at[me], l_sem.at[0])
     own_items = pltpu.make_async_copy(items_ref, item_v, l_sem.at[1])
     own_fresh = pltpu.make_async_copy(fresh_ref, fresh_v.at[0], l_sem.at[2])
+    small = [
+        pltpu.make_async_copy(src, dst, l_sem.at[3 + i])
+        for i, (src, dst) in enumerate(((ages_hbm, ages_ref), (fages_hbm, fages_ref), (probes_hbm, probes_ref)))
+    ]
+    for copy in small:
+        copy.start()
     own_q.start()
     own_items.start()
     own_fresh.start()
@@ -107,7 +118,7 @@
         device_id=(1 - rep, me), device_id_type=MESH,
     )
     sibling_age = pltpu.make_async_remote_copy(
-        src_ref=fages_ref, dst_ref=fage_v, send_sem=f_sem.at[2], recv_sem=f_sem.at[3],
+        src_ref=fages_hbm, dst_ref=fage_v, send_sem=f_sem.at[2], recv_sem=f_sem.at[3],
         device_id=(1 - rep, me), device_id_type=MESH,
     )
 
@@ -125,6 +136,9 @@
     sibling_age.start()
     sibling.start()
 
+    for copy in small:
+        copy.wait()
+
     def spread(row):
         return jnp.transpose(jnp.broadcast_to(row.astype(jnp.float32), (ITEMS_BLOCK, ITEMS_BLOCK)))
 
@@ -133,7 +147,7 @@
         age_v[pl.ds(pl.multiple_of(k * ITEMS_BLOCK, ITEMS_BLOCK), ITEMS_BLOCK), :] = spread(ages_ref[pl.ds(k, 1), :])
 
     rate_v[me] = rate_s[...]
-    probes = jnp.transpose(probes_ref[...])
+    probes = probes_ref[...]
 
     def place_step(l, acc):
         return jnp.where(probes == l, place_ref[l], acc)
@@ -166,14 +180,6 @@
 
     @pl.loop(0, A + 1)
     def _(j):
-        @pl.when(j + 1 < A)
-        def _():
-            wait_block(at(j + 1, 0, 0))
-            for dc in range(1, C):
-                c_send(j + 1, dc).start()
-            for db in range(1, B):
-                b_send(j + 1, db).start()
-
         @pl.when(j < A)
         def _():
             for dc in range(1, C):
@@ -185,6 +191,14 @@
                 for dc in range(1, C):
                     hc_send(j, db, dc).start()
 
+        @pl.when(j + 1 < A)
+        def _():
+            wait_block(at(j + 1, 0, 0))
+            for dc in range(1, C):
+                c_send(j + 1, dc).start()
+            for db in range(1, B):
+                b_send(j + 1, db).start()
+
         @pl.loop(0, pairs)
         def _(t):
             jj = jnp.where(t < front, j, j - 1)
@@ -251,10 +265,10 @@
     zero = jnp.zeros((blocks, rows), jnp.float32)
     outs, fr = lax.fori_loop(
         0, n, collect,
-        (tuple(zero for _ in range(probes_ref.shape[1])), jnp.zeros((fresh_blocks, rows), jnp.float32)),
+        (tuple(zero for _ in range(probes_ref.shape[0])), jnp.zeros((fresh_blocks, rows), jnp.float32)),
     )
     out_ref[...] = jnp.transpose(jnp.concatenate(outs, axis=0))
-    fout_ref[...] = jnp.transpose(fr)
+    fout_ref[...] = fr
 
     for j in range(A):
         for dc in range(1, C):
@@ -292,30 +306,31 @@
         ((2, fresh_n, width), bf), ((fresh_rows, ITEMS_BLOCK), i32),
         ((item_n + fresh_n, ITEMS_BLOCK), f32), ((8, rows), f32), ((n, 8, rows), f32),
         ((probes.shape[1], rows), i32), ((n, res_rows, rows), f32), ((n, res_rows, rows), f32),
+        ((probes.shape[1], rows), i32), ((main_rows, ITEMS_BLOCK), i32), ((fresh_rows, ITEMS_BLOCK), i32),
     ]
-    used = sum(math.prod(shape) * jnp.dtype(kind).itemsize for shape, kind in scratch)
     dma = pltpu.SemaphoreType.DMA
     smem, vmem, hbm = (pl.BlockSpec(memory_space=m) for m in (pltpu.SMEM, pltpu.VMEM, pl.ANY))
-    return pl.pallas_call(
+    best, fresh = pl.pallas_call(
         functools.partial(kernel, n, dims, lists_n, per_dev),
         out_shape=(
             jax.ShapeDtypeStruct((rows, probes.shape[1] * (main_rows // per_dev)), f32),
-            jax.ShapeDtypeStruct((rows, fresh_rows), f32),
+            jax.ShapeDtypeStruct((fresh_rows, rows), f32),
         ),
-        in_specs=[smem, smem, vmem, vmem, vmem, vmem, hbm, hbm, hbm],
+        in_specs=[smem, smem, vmem] + [hbm] * 6,
         out_specs=(vmem, vmem),
         scratch_shapes=[pltpu.VMEM(shape, kind) for shape, kind in scratch] + [
             dma((A,)), dma((A, B)), dma((A, C)), dma((A, C, B)), dma((A, B, C)),
-            dma((n,)), dma((n,)), dma((n, 2)), dma((n,)), dma((n,)), dma((4,)), dma((3,)),
+            dma((n,)), dma((n,)), dma((n, 2)), dma((n,)), dma((n,)), dma((4,)), dma((6,)),
         ],
         compiler_params=pltpu.CompilerParams(
-            collective_id=0, has_side_effects=True, vmem_limit_bytes=used + (10 << 20)
+            collective_id=0, has_side_effects=True, vmem_limit_bytes=63 << 20
         ),
     )(
-        owner, list_place, rates.reshape(1, rows), probes,
+        owner, list_place, rates.reshape(1, rows), probes.T,
         ages.reshape(main_rows, ITEMS_BLOCK), fresh_ages.reshape(fresh_rows, ITEMS_BLOCK),
         queries, items, fresh_items,
     )
+    return best, fresh.T
 
 
 def solution(mesh):

time: 74.3 us -> 59.2 us (0.80)
  Pallas kernels: 62.7 us -> 54.9 us
  local copies, waits for them, and re-layouts: 9.9 us -> 2.74 us
    pallas_call x1, Pallas kernels: 62.7 us -> 54.9 us  [shards(): pl.pallas_call(functools.partial(kernel, n, dims, lists_n, per_dev), out_...]
    unnamed x16 -> x2, local copies, waits for them, and re-layouts: 9.24 us -> 2.74 us
where the time goes in v2:
time: 59.2 us; the launch traced here: 58.9 us
  Pallas kernels  54.9 us (93%)
  local copies, waits for them, and re-layouts  2.74 us (5%)
  between operations  1.29 us (2%)
    pallas_call x1, Pallas kernels, shards(): pl.pallas_call(functools.partial(kernel, n, dims, lists_n, per_dev), out_...  54.9 us
    unnamed x2, local copies, waits for them, and re-layouts  2.74 us

profile of v2, /device:TPU:0, one launch (start us, length us, event | category | flops | bytes accessed | tf_op | source)
XLA Modules:
  0.0 58.9 jit_solution(14370751349964718035)
XLA Ops:
  1.3 54.9 %shard_map.104 = (f32[128,128]{1,0:T(8,128)}, f32[8,128]{1,0:T(8,128)}) custom-call(s32[1]{0:T(128)S(6)} %copy.13.owner_ref, s32[32]{0:T(128)} %place_ref.1, bf16[1,128]{1,0:T(2,128)(2,1)} %bitcast.9, s32[8,128]{1,0:T(8,128)} %bitcast.6, s32[32,128]{1,0:T(8,128)} %bitcast.5, s32[8,128]{1,0:T(8,128)} %bitcast.7, bf16[128,768]{1,0:T(8,128)(2,1)} %q_ref.1, ...), custom_call_target="tpu_custom_call" | custom-call | tf_op jit(solution)/shard_map/pallas_call | solution.py:313
  56.2 1.5 %copy.14 = f32[128,128]{1,0:T(8,128)} copy(f32[128,128]{1,0:T(8,128)} %get-tuple-element.8) | data formatting | bytes 131072
  57.7 1.3 %copy.15 = f32[128,8]{0,1:T(8,128)} copy(f32[128,8]{0,1:T(8,128)} %bitcast.8) | data formatting | bytes 8192
